TPU v7x, 32 devices: a whole 2x2x4 slice. The times are simulated.
32 devices in a mesh: tensor: 4 (over y, core), dp: 8 (over z, x).
Axes of the slice: x: 2, y: 2, z: 4, core: 2. Of those that a mesh axis runs over, the one named last changes fastest.
Arguments:
- hidden: bfloat16 [6144, 14336], P('dp', 'tensor'), may hold values from -6 to 6
- upstream: bfloat16 [6144, 4096], P('dp'), may hold values from -4 to 4
- head_weight: bfloat16 [14, 4096], replicated, may hold values from -2 to 2
- class_probs: float32 [6144, 14], P('dp'), as said below
- teacher_votes: int32 [6144, 14], P('dp'), may hold values from 0 to 7
- clean_flag: int32 [6144], P('dp'), may hold values from 0 to 1, as said below
Outputs:
- reweighted: bfloat16 [4096, 14336], P('dp', 'tensor')
Inputs may be any that keep to these rules, and one draw needn't show every extreme that they name: In each aligned block of 768 examples exactly 16 have clean_flag 1. `class_probs`: every row is positive and sums to one.
All inputs are finite; a program needn't handle non-finite values.
Results may differ from a plain program's by a relative error of at most 0.019.
Values may be sent and summed in bfloat16 or wider, within the bound.
A program may use at most 128 MiB of HBM per device.

v0:
```python
import jax
import jax.numpy as jnp
from jax import lax
from jax.sharding import PartitionSpec as P

CLEAN_DEV = 16
CHUNKS = 4


def gram(left, right):
    return lax.dot_general(
        left, right, (((1,), (1,)), ((), ())), preferred_element_type=jnp.float32
    )


def gradient(upstream, errors, head_weight):
    first = lax.reduce_precision(errors, 8, 7)
    second = lax.reduce_precision(errors - first, 8, 7)
    third = errors - first - second
    terms = jnp.concatenate([first, second, third], axis=1).astype(jnp.bfloat16)
    heads = jnp.concatenate([head_weight] * 3, axis=0)
    product = jnp.dot(terms, heads, preferred_element_type=jnp.float32)
    return (upstream.astype(jnp.float32) + product).astype(jnp.bfloat16)


def exchange(array, bit):
    size = lax.axis_size("dp")
    return lax.ppermute(array, "dp", [(i, i ^ bit) for i in range(size)])


def body(hidden, upstream, head_weight, class_probs, teacher_votes, clean_flag):
    examples, units = hidden.shape
    width = upstream.shape[1]
    classes = class_probs.shape[1]
    groups = lax.axis_size("dp")
    me = lax.axis_index("dp")
    high = groups // 4
    rows = width // groups
    part = rows // CHUNKS
    low_bit, mid_bit, high_index = (me % 2, me // 2 % 2, me // 4)
    partner_hidden = exchange(hidden, 2)
    labels = jnp.argmax(teacher_votes, axis=1)
    onehot = (labels[:, None] == jnp.arange(classes, dtype=jnp.int32)[None, :]).astype(jnp.float32)
    grad_out = gradient(upstream, class_probs - onehot, head_weight)
    place = jnp.arange(examples, dtype=jnp.int32)
    order = jnp.sum(jnp.where(place[None, :] <= place[:, None], clean_flag[None, :], 0), axis=1)
    slots = jnp.arange(1, CLEAN_DEV + 1, dtype=jnp.int32)
    pick = ((order[None, :] == slots[:, None]) & (clean_flag[None, :] == 1)).astype(jnp.bfloat16)
    clean_hidden = jnp.dot(pick, hidden, preferred_element_type=jnp.float32).astype(jnp.bfloat16)
    clean_grad = jnp.dot(pick, grad_out, preferred_element_type=jnp.float32).astype(jnp.bfloat16)
    all_hidden = lax.all_gather(clean_hidden, "dp", axis=0, tiled=True)
    all_grad = lax.all_gather(clean_grad, "dp", axis=0, tiled=True)
    split = grad_out.reshape(examples, high, 2, 2 * rows)
    own_half = lax.dynamic_index_in_dim(split, mid_bit, 2, keepdims=False)
    other_half = lax.dynamic_index_in_dim(split, 1 - mid_bit, 2, keepdims=False)
    other_half = other_half.reshape(examples, width // 2)
    partner_grad = exchange(other_half, 2)
    own_grad = own_half.reshape(examples, width // 2)
    local_scores = jnp.sum(gram(hidden, all_hidden) * gram(grad_out, all_grad), axis=1)
    scores = lax.psum(local_scores, "tensor")
    clean_total = groups * CLEAN_DEV
    noisy_total = groups * (examples - CLEAN_DEV)
    units_total = units * lax.axis_size("tensor")
    scores = scores / jnp.sqrt(
        jnp.float32(units_total) * jnp.float32(width) * jnp.float32(clean_total)
    )
    weights = (
        jax.nn.softplus(scores)
        * (1 - clean_flag).astype(jnp.float32)
        / jnp.sqrt(jnp.float32(noisy_total))
    )
    both_weights = jnp.concatenate([weights, exchange(weights, 2)])
    both_hidden = jnp.concatenate([hidden, partner_hidden], axis=0)
    both_grad = jnp.concatenate([own_grad, partner_grad], axis=0)
    weighted = (both_weights[:, None] * both_grad.astype(jnp.float32)).astype(jnp.bfloat16)
    weighted = weighted.reshape(2 * examples, high, 2, CHUNKS, part)
    keep_all = lax.dynamic_index_in_dim(weighted, low_bit, 2, keepdims=False)
    send_all = lax.dynamic_index_in_dim(weighted, 1 - low_bit, 2, keepdims=False)

    def product(block):
        return lax.dot_general(
            block.reshape(2 * examples, high * part),
            both_hidden,
            (((0,), (0,)), ((), ())),
            preferred_element_type=jnp.float32,
        )

    pieces = []
    for chunk in range(CHUNKS):
        sent = product(send_all[:, :, chunk]).astype(jnp.bfloat16)
        arrived = exchange(sent, 1)
        total = (product(keep_all[:, :, chunk]) + arrived.astype(jnp.float32)).astype(jnp.bfloat16)
        size, bit = (high, 4 * (high // 2))
        while size > 1:
            total = total.reshape(2, size // 2 * part, units)
            upper = high_index // (size // 2) % 2
            keep = lax.dynamic_index_in_dim(total, upper, 0, keepdims=False)
            give = lax.dynamic_index_in_dim(total, 1 - upper, 0, keepdims=False)
            arrived = exchange(give, bit)
            total = (keep.astype(jnp.float32) + arrived.astype(jnp.float32)).astype(jnp.bfloat16)
            size, bit = (size // 2, bit // 2)
        pieces.append(total)
    return jnp.concatenate(pieces, axis=0)


def solution(mesh):
    return jax.shard_map(
        body,
        mesh=mesh,
        in_specs=(P("dp", "tensor"), P("dp", None), P(), P("dp", None), P("dp", None), P("dp")),
        out_specs=P("dp", "tensor"),
        check_vma=False,
    )
```

profile of v0, /device:TPU:0, one launch (start us, length us, event | category | flops | bytes accessed | tf_op | source)
XLA Modules:
  0.0 530.3 jit_solution(115440441244654834)
XLA Ops:
  6.5 3.0 collective-permute-start.2
  12.6 4.8 add_convert_fusion
  17.4 2.6 copy-done.2
  21.8 11.1 %reshape.48 = bf16[768,2,2,1024]{3,2,1,0:T(2,128)(2,1)} reshape(bf16[768,4096]{1,0:T(8,128)(2,1)} %copy-done.2) | data formatting | bytes 12582912 | tf_op jit(solution)/shard_map/reshape | solution.py:53
  32.9 15.9 %constant_dynamic-slice_fusion.3 = (bf16[768,2,1,1024]{3,2,1,0:T(2,128)(2,1)}, bf16[768,2,1,1024]{3,2,1,0:T(2,128)(2,1)}) fusion(bf16[768,2,2,1024]{3,2,1,0:T(2,128)(2,1)} %reshape.48, s32[]{:T(128)S(6)} %select_n.75, s32[]{:T(128)S(6)} %select_n.76), kind=kLoop, calls=%fused_computation.68 | loop fusion | bytes 12582920 | tf_op jit(solution)/shard_map/jit(dynamic_index_in_dim)/dynamic_slice | solution.py:54
  48.8 15.1 %copy.34 = bf16[768,2,1,1024]{0,3,1,2:T(8,128)(2,1)} copy(bf16[768,2,1,1024]{3,2,1,0:T(2,128)(2,1)} %get-tuple-element.10) | data formatting | bytes 6291456
  64.0 3.4 convolution_convert_fusion.5
  67.4 170.3 %all_gather.6 = bf16[128,3584]{1,0:T(8,128)(2,1)S(1)} all-gather(bf16[16,3584]{1,0:T(8,128)(2,1)S(1)} %convolution_convert_fusion.5), channel_id=1, replica_groups=mesh['tensor'=4,'dp'=8] {'dp'}, dimensions={0}, use_global_device_ids=true | all-gather | bytes 1032192 | tf_op jit(solution)/shard_map/all_gather | solution.py:51
  237.8 5.2 fusion.32
  243.0 4.4 fusion.9
  247.4 5.7 %psum.7 = f32[768]{0:T(1024)S(1)} all-reduce(f32[768]{0:T(1024)S(1)} %fusion.9), channel_id=1, replica_groups=mesh['tensor'=4,'dp'=8] {'tensor'}, use_global_device_ids=true, to_apply=%region_3.4 | all-reduce | flops 768 | bytes 6144 | tf_op jit(solution)/shard_map/psum | solution.py:60
  253.2 5.3 %constant_dynamic-update-slice_fusion.1 = bf16[1536,3584]{1,0:T(8,128)(2,1)} fusion(bf16[768,3584]{1,0:T(8,128)(2,1)} %param.6), kind=kLoop, calls=%fused_computation.62 | loop fusion | bytes 11010048
  258.5 13.3 %copy.33 = bf16[768,2,1,1024]{0,3,1,2:T(8,128)(2,1)S(1)} copy(bf16[768,2,1,1024]{3,2,1,0:T(2,128)(2,1)} %get-tuple-element.9) | data formatting | bytes 6291456
  271.9 3.2 multiply_convert_fusion
  275.1 3.3 constant_dynamic-slice_fusion
  278.4 3.5 copy.25
  283.6 2.4 copy.26
  290.8 3.5 copy.23
  300.4 5.4 %constant_dynamic-update-slice_fusion = bf16[1536,3584]{1,0:T(8,128)(2,1)} fusion(bf16[1536,3584]{1,0:T(8,128)(2,1)} %constant_dynamic-update-slice_fusion.1, bf16[768,3584]{1,0:T(8,128)(2,1)} %collective-permute-done.2), kind=kLoop, calls=%fused_computation.61 | loop fusion | bytes 11010048 | tf_op jit(solution)/shard_map/concatenate | solution.py:73
  305.8 7.3 %convolution_convert_fusion.2 = bf16[256,3584]{1,0:T(8,128)(2,1)S(1)} fusion(bf16[1536,256]{0,1:T(8,128)(2,1)S(1)} %bitcast.83, bf16[1536,3584]{1,0:T(8,128)(2,1)} %constant_dynamic-update-slice_fusion), kind=kOutput, calls=%fused_computation.12 | convolution fusion | flops 2819489792 | bytes 13631488 | tf_op jit(solution)/shard_map/dot_general | solution.py:81
  313.2 3.0 convolution_convert_fusion.3
  318.3 3.0 convolution_convert_fusion
  321.4 3.0 convolution_convert_fusion.1
  326.5 32.7 %collective-permute-done.3 = bf16[256,3584]{1,0:T(8,128)(2,1)S(1)} collective-permute-done((bf16[256,3584]{1,0:T(8,128)(2,1)S(1)}, bf16[256,3584]{1,0:T(8,128)(2,1)S(1)}, u32[]{:S(2)}, u32[]{:S(2)}) %collective-permute-start.3) | collective-permute-done | bytes 1835040 | tf_op jit(solution)/shard_map/ppermute | solution.py:28
  359.2 3.0 fusion
  363.5 35.0 %collective-permute-done.5 = bf16[256,3584]{1,0:T(8,128)(2,1)S(1)} collective-permute-done((bf16[256,3584]{1,0:T(8,128)(2,1)S(1)}, bf16[256,3584]{1,0:T(8,128)(2,1)S(1)}, u32[]{:S(2)}, u32[]{:S(2)}) %collective-permute-start.5) | collective-permute-done | bytes 1835040 | tf_op jit(solution)/shard_map/ppermute | solution.py:28
  398.5 3.3 fusion.1
  403.1 34.7 %collective-permute-done.7 = bf16[256,3584]{1,0:T(8,128)(2,1)S(1)} collective-permute-done((bf16[256,3584]{1,0:T(8,128)(2,1)S(1)}, bf16[256,3584]{1,0:T(8,128)(2,1)S(1)}, u32[]{:S(2)}, u32[]{:S(2)}) %collective-permute-start.7) | collective-permute-done | bytes 1835040 | tf_op jit(solution)/shard_map/ppermute | solution.py:28
  437.8 3.1 fusion.2
  442.2 33.9 %collective-permute-done.9 = bf16[256,3584]{1,0:T(8,128)(2,1)S(1)} collective-permute-done((bf16[256,3584]{1,0:T(8,128)(2,1)S(1)}, bf16[256,3584]{1,0:T(8,128)(2,1)S(1)}, u32[]{:S(2)}, u32[]{:S(2)}) %collective-permute-start.9) | collective-permute-done | bytes 1835040 | tf_op jit(solution)/shard_map/ppermute | solution.py:28
  476.1 3.1 fusion.3
  482.4 38.9 %collective-permute-done.10 = bf16[128,3584]{1,0:T(8,128)(2,1)S(1)} collective-permute-done((bf16[128,3584]{1,0:T(8,128)(2,1)S(1)}, bf16[128,3584]{1,0:T(8,128)(2,1)S(1)}, u32[]{:S(2)}, u32[]{:S(2)}) %collective-permute-start.10) | collective-permute-done | bytes 917536 | tf_op jit(solution)/shard_map/ppermute | solution.py:28
  (72 shorter events, 30.8 us)
Async XLA Ops:
  6.5 4.6 copy-start
  6.5 231.2 %all-gather.2.cloned.1.call-start = ((), (), s32[]{:S(2)}) async-start(), calls=%async_computation | async-start | bytes 1179648 | tf_op jit(solution)/shard_map/all_gather | solution.py:52
  6.5 293.8 %collective-permute-start.2 = (bf16[768,3584]{1,0:T(8,128)(2,1)}, bf16[768,3584]{1,0:T(8,128)(2,1)}, u32[]{:S(2)}, u32[]{:S(2)}) collective-permute-start(bf16[768,3584]{1,0:T(8,128)(2,1)} %param.6), channel_id=1, source_target_pairs={{0,2},{1,3},{2,0},{3,1},{4,6},{5,7},{6,4},{7,5},{8,10},{9,11},{10,... | collective-permute-start | bytes 16515080 | tf_op jit(solution)/shard_map/ppermute | solution.py:28
  17.4 2.6 copy-start.2
  63.9 208.0 %collective-permute-start.1 = (bf16[768,2048]{0,1:T(8,128)(2,1)}, bf16[768,2048]{0,1:T(8,128)(2,1)}, u32[]{:S(2)}, u32[]{:S(2)}) collective-permute-start(bf16[768,2048]{0,1:T(8,128)(2,1)} %bitcast.2), channel_id=1, source_target_pairs={{0,2},{1,3},{2,0},{3,1},{4,6},{5,7},{6,4},{7,5},{8,10},{9,11},{10,... | collective-permute-start | bytes 9437192 | tf_op jit(solution)/shard_map/ppermute | solution.py:28
  243.0 10.1 %copy-start.13 = (s32[768]{0:T(1024)S(1)}, s32[768]{0:T(1024)}, u32[]{:S(2)}) copy-start(s32[768]{0:T(1024)} %param.11) | copy-start | bytes 9220
  253.1 18.7 %collective-permute-start = (f32[768]{0:T(1024)S(1)}, f32[768]{0:T(1024)S(1)}, u32[]{:S(2)}, u32[]{:S(2)}) collective-permute-start(f32[768]{0:T(1024)S(1)} %fusion.28), channel_id=1, source_target_pairs={{0,2},{1,3},{2,0},{3,1},{4,6},{5,7},{6,4},{7,5},{8,10},{9,11},{10,... | collective-permute-start | bytes 9224 | tf_op jit(solution)/shard_map/ppermute | solution.py:28
  283.6 4.7 copy-start.5
  283.6 5.9 %copy-start.3 = (bf16[1536,2,1,128]{3,0,2,1:T(8,128)(2,1)S(1)}, bf16[1536,2,1,128]{3,0,2,1:T(8,128)(2,1)}, u32[]{:S(2)}) copy-start(bf16[1536,2,1,128]{3,0,2,1:T(8,128)(2,1)} %get-tuple-element.14) | copy-start | bytes 2359300
  296.0 3.8 copy-start.6
  296.0 4.1 copy-start.4
  300.4 5.5 %copy-start.12 = (bf16[1536,2,1,128]{0,3,1,2:T(8,128)(2,1)S(1)}, bf16[1536,2,1,128]{0,3,1,2:T(8,128)(2,1)}, u32[]{:S(2)}) copy-start(bf16[1536,2,1,128]{0,3,1,2:T(8,128)(2,1)} %copy.28) | copy-start | bytes 2359300
  305.8 7.3 %copy-start.7 = (bf16[1536,3584]{1,0:T(8,128)(2,1)S(1)}, bf16[1536,3584]{1,0:T(8,128)(2,1)}, u32[]{:S(2)}) copy-start(bf16[1536,3584]{1,0:T(8,128)(2,1)} %constant_dynamic-update-slice_fusion) | copy-start | bytes 33030148
  305.8 7.4 %copy-start.11 = (bf16[1536,2,1,128]{0,3,1,2:T(8,128)(2,1)S(1)}, bf16[1536,2,1,128]{0,3,1,2:T(8,128)(2,1)}, u32[]{:S(2)}) copy-start(bf16[1536,2,1,128]{0,3,1,2:T(8,128)(2,1)} %copy.26) | copy-start | bytes 2359300
  313.2 5.1 copy-start.8
  316.2 43.0 %collective-permute-start.3 = (bf16[256,3584]{1,0:T(8,128)(2,1)S(1)}, bf16[256,3584]{1,0:T(8,128)(2,1)S(1)}, u32[]{:S(2)}, u32[]{:S(2)}) collective-permute-start(bf16[256,3584]{1,0:T(8,128)(2,1)S(1)} %convolution_convert_fusion.3), channel_id=1, source_target_pairs={{0,1},{1,0},{2,3},{3,2},{4,5},{5,4},{6,7},{7,6},{8,9},{9,8},{10,11... | collective-permute-start | bytes 5505032 | tf_op jit(solution)/shard_map/ppermute | solution.py:28
  316.3 82.2 %collective-permute-start.5 = (bf16[256,3584]{1,0:T(8,128)(2,1)S(1)}, bf16[256,3584]{1,0:T(8,128)(2,1)S(1)}, u32[]{:S(2)}, u32[]{:S(2)}) collective-permute-start(bf16[256,3584]{1,0:T(8,128)(2,1)S(1)} %convolution_convert_fusion.2), channel_id=1, source_target_pairs={{0,1},{1,0},{2,3},{3,2},{4,5},{5,4},{6,7},{7,6},{8,9},{9,8},{10,11... | collective-permute-start | bytes 5505032 | tf_op jit(solution)/shard_map/ppermute | solution.py:28
  318.3 3.0 copy-start.9
  321.4 37.8 %copy-start.10 = (bf16[1536,2,1,128]{0,3,1,2:T(8,128)(2,1)S(1)}, bf16[1536,2,1,128]{0,3,1,2:T(8,128)(2,1)}, u32[]{:S(2)}) copy-start(bf16[1536,2,1,128]{0,3,1,2:T(8,128)(2,1)} %copy.24) | copy-start | bytes 2359300
  324.4 113.5 %collective-permute-start.7 = (bf16[256,3584]{1,0:T(8,128)(2,1)S(1)}, bf16[256,3584]{1,0:T(8,128)(2,1)S(1)}, u32[]{:S(2)}, u32[]{:S(2)}) collective-permute-start(bf16[256,3584]{1,0:T(8,128)(2,1)S(1)} %convolution_convert_fusion.1), channel_id=1, source_target_pairs={{0,1},{1,0},{2,3},{3,2},{4,5},{5,4},{6,7},{7,6},{8,9},{9,8},{10,11... | collective-permute-start | bytes 5505032 | tf_op jit(solution)/shard_map/ppermute | solution.py:28
  324.5 151.5 %collective-permute-start.9 = (bf16[256,3584]{1,0:T(8,128)(2,1)S(1)}, bf16[256,3584]{1,0:T(8,128)(2,1)S(1)}, u32[]{:S(2)}, u32[]{:S(2)}) collective-permute-start(bf16[256,3584]{1,0:T(8,128)(2,1)S(1)} %convolution_convert_fusion), channel_id=1, source_target_pairs={{0,1},{1,0},{2,3},{3,2},{4,5},{5,4},{6,7},{7,6},{8,9},{9,8},{10,11... | collective-permute-start | bytes 5505032 | tf_op jit(solution)/shard_map/ppermute | solution.py:28
  362.3 117.8 %collective-permute-start.4 = (bf16[128,3584]{1,0:T(8,128)(2,1)S(1)}, bf16[128,3584]{1,0:T(8,128)(2,1)S(1)}, u32[]{:S(2)}, u32[]{:S(2)}) collective-permute-start(bf16[128,3584]{1,0:T(8,128)(2,1)S(1)} %dynamic-slice_bitcast_fusion.3), channel_id=1, source_target_pairs={{0,4},{1,5},{2,6},{3,7},{4,0},{5,1},{6,2},{7,3},{8,12},{9,13},{10,... | collective-permute-start | bytes 2752520 | tf_op jit(solution)/shard_map/ppermute | solution.py:28
  401.9 78.4 %collective-permute-start.6 = (bf16[128,3584]{1,0:T(8,128)(2,1)S(1)}, bf16[128,3584]{1,0:T(8,128)(2,1)S(1)}, u32[]{:S(2)}, u32[]{:S(2)}) collective-permute-start(bf16[128,3584]{1,0:T(8,128)(2,1)S(1)} %dynamic-slice_bitcast_fusion.2), channel_id=1, source_target_pairs={{0,4},{1,5},{2,6},{3,7},{4,0},{5,1},{6,2},{7,3},{8,12},{9,13},{10,... | collective-permute-start | bytes 2752520 | tf_op jit(solution)/shard_map/ppermute | solution.py:28
  441.0 41.2 %collective-permute-start.8 = (bf16[128,3584]{1,0:T(8,128)(2,1)S(1)}, bf16[128,3584]{1,0:T(8,128)(2,1)S(1)}, u32[]{:S(2)}, u32[]{:S(2)}) collective-permute-start(bf16[128,3584]{1,0:T(8,128)(2,1)S(1)} %dynamic-slice_bitcast_fusion.1), channel_id=1, source_target_pairs={{0,4},{1,5},{2,6},{3,7},{4,0},{5,1},{6,2},{7,3},{8,12},{9,13},{10,... | collective-permute-start | bytes 2752520 | tf_op jit(solution)/shard_map/ppermute | solution.py:28
  479.2 42.1 %collective-permute-start.10 = (bf16[128,3584]{1,0:T(8,128)(2,1)S(1)}, bf16[128,3584]{1,0:T(8,128)(2,1)S(1)}, u32[]{:S(2)}, u32[]{:S(2)}) collective-permute-start(bf16[128,3584]{1,0:T(8,128)(2,1)S(1)} %dynamic-slice_bitcast_fusion), channel_id=1, source_target_pairs={{0,4},{1,5},{2,6},{3,7},{4,0},{5,1},{6,2},{7,3},{8,12},{9,13},{10,... | collective-permute-start | bytes 2752520 | tf_op jit(solution)/shard_map/ppermute | solution.py:28
  521.3 2.2 copy-start.1
Sparse Core Ops, SparseCore 0:
  21.8 45.1 all-gather.1
where the time goes:
time: 532 us; the launch traced here: 530 us
  waiting for transfers between devices  177 us (33%)
  blocking collectives  176 us (33%)
  local copies, waits for them, and re-layouts  94.5 us (18%)
  matrix products  48.3 us (9%)
  between operations  13.8 us (3%)
  starting transfers between devices  11.9 us (2%)
  other arithmetic  9.02 us (2%)
    ppermute x11, waiting for transfers between devices, exchange(): return lax.ppermute(array, 'dp', [(i, i ^ bit) for i in range(size)])  177 us
    all_gather x1, blocking collectives, body(): all_hidden = lax.all_gather(clean_hidden, 'dp', axis=0, tiled=True)  170 us
    unnamed x31, local copies, waits for them, and re-layouts  36.5 us
    dot_general x8, matrix products, product(): lax.dot_general(block.reshape(2 * examples, high * part), both_hidden, ((...  28.7 us
    dynamic_slice x1, local copies, waits for them, and re-layouts, body(): own_half = lax.dynamic_index_in_dim(split, mid_bit, 2, keepdims=False)  15.9 us
    ppermute x11, starting transfers between devices, exchange(): return lax.ppermute(array, 'dp', [(i, i ^ bit) for i in range(size)])  11.9 us
    reshape x1, local copies, waits for them, and re-layouts, body(): split = grad_out.reshape(examples, high, 2, 2 * rows)  11.1 us
  transfers between devices with their start and end apart: 12, of which 6 were waited for; matrix products, arithmetic and copies ran while one was open for 25% of the time, Pallas kernels for 0%

commit v1 on v0

--- a/solution.py
+++ b/solution.py
@@ -48,8 +48,13 @@
     pick = ((order[None, :] == slots[:, None]) & (clean_flag[None, :] == 1)).astype(jnp.bfloat16)
     clean_hidden = jnp.dot(pick, hidden, preferred_element_type=jnp.float32).astype(jnp.bfloat16)
     clean_grad = jnp.dot(pick, grad_out, preferred_element_type=jnp.float32).astype(jnp.bfloat16)
-    all_hidden = lax.all_gather(clean_hidden, "dp", axis=0, tiled=True)
-    all_grad = lax.all_gather(clean_grad, "dp", axis=0, tiled=True)
+    all_hidden, all_grad = jnp.split(
+        lax.all_gather(
+            jnp.concatenate([clean_hidden, clean_grad], axis=1), "dp", axis=0, tiled=True
+        ),
+        [clean_hidden.shape[1]],
+        axis=1,
+    )
     split = grad_out.reshape(examples, high, 2, 2 * rows)
     own_half = lax.dynamic_index_in_dim(split, mid_bit, 2, keepdims=False)
     other_half = lax.dynamic_index_in_dim(split, 1 - mid_bit, 2, keepdims=False)

time: 532 us -> 494 us (0.929)
  blocking collectives: 176 us -> 7.45 us
  waiting for transfers between devices: 177 us -> 298 us
  starting transfers between devices: 11.9 us -> 21.7 us
    all_gather x1 -> x0, blocking collectives: 170 us -> none  [body(): all_hidden = lax.all_gather(clean_hidden, 'dp', axis=0, tiled=True)]
    ppermute x11, waiting for transfers between devices: 177 us -> 276 us  [exchange(): return lax.ppermute(array, 'dp', [(i, i ^ bit) for i in range(size)])]
    all_gather x1, waiting for transfers between devices: 0.01 us -> 21.6 us  [body(): lax.all_gather(jnp.concatenate([clean_hidden, clean_grad], axis=1), 'dp',...]
    ppermute x11, starting transfers between devices: 11.9 us -> 21.7 us  [exchange(): return lax.ppermute(array, 'dp', [(i, i ^ bit) for i in range(size)])]
    unnamed x31 -> x33, local copies, waits for them, and re-layouts: 36.5 us -> 36.5 us
  transfers between devices with their start and end apart: 12 -> 12, of which waited for: 6 -> 7; matrix products, arithmetic and copies ran while one was open for 25% -> 24% of each run, Pallas kernels for 0% -> 0%
where the time goes in v1:
time: 494 us; the launch traced here: 493 us
  waiting for transfers between devices  298 us (60%)
  local copies, waits for them, and re-layouts  94.6 us (19%)
  matrix products  47.7 us (10%)
  starting transfers between devices  21.7 us (4%)
  between operations  13.7 us (3%)
  other arithmetic  9.82 us (2%)
  blocking collectives  7.45 us (2%)
    ppermute x11, waiting for transfers between devices, exchange(): return lax.ppermute(array, 'dp', [(i, i ^ bit) for i in range(size)])  276 us
    unnamed x33, local copies, waits for them, and re-layouts  36.5 us
    dot_general x8, matrix products, product(): lax.dot_general(block.reshape(2 * examples, high * part), both_hidden, ((...  28.7 us
    ppermute x11, starting transfers between devices, exchange(): return lax.ppermute(array, 'dp', [(i, i ^ bit) for i in range(size)])  21.7 us
    all_gather x1, waiting for transfers between devices, body(): lax.all_gather(jnp.concatenate([clean_hidden, clean_grad], axis=1), 'dp',...  21.6 us
    dynamic_slice x1, local copies, waits for them, and re-layouts, body(): own_half = lax.dynamic_index_in_dim(split, mid_bit, 2, keepdims=False)  15.9 us
    reshape x1, local copies, waits for them, and re-layouts, body(): split = grad_out.reshape(examples, high, 2, 2 * rows)  11.2 us
    dot_general x2, matrix products, gram(): lax.dot_general(left, right, (((1,), (1,)), ((), ())), preferred_element_...  9.96 us
  transfers between devices with their start and end apart: 12, of which 7 were waited for; matrix products, arithmetic and copies ran while one was open for 24% of the time, Pallas kernels for 0%

profile of v1, /device:TPU:0, one launch (start us, length us, event | category | flops | bytes accessed | tf_op | source)
XLA Modules:
  0.0 492.6 jit_solution(17213333851744844796)
XLA Ops:
  9.6 3.4 convolution_convert_fusion.5
  13.0 4.6 add_convert_fusion
  22.0 3.1 collective-permute-start.2
  25.1 11.2 %reshape.48 = bf16[768,2,2,1024]{3,2,1,0:T(2,128)(2,1)} reshape(bf16[768,4096]{1,0:T(8,128)(2,1)} %copy-done.2) | data formatting | bytes 12582912 | tf_op jit(solution)/shard_map/reshape | solution.py:58
  36.3 15.9 %constant_dynamic-slice_fusion.3 = (bf16[768,2,1,1024]{3,2,1,0:T(2,128)(2,1)}, bf16[768,2,1,1024]{3,2,1,0:T(2,128)(2,1)}) fusion(bf16[768,2,2,1024]{3,2,1,0:T(2,128)(2,1)} %reshape.48, s32[]{:T(128)S(6)} %select_n.75, s32[]{:T(128)S(6)} %select_n.76), kind=kLoop, calls=%fused_computation.72 | loop fusion | bytes 12582920 | tf_op jit(solution)/shard_map/jit(dynamic_index_in_dim)/dynamic_slice | solution.py:59
  52.2 15.2 %copy.34 = bf16[768,2,1,1024]{0,3,1,2:T(8,128)(2,1)} copy(bf16[768,2,1,1024]{3,2,1,0:T(2,128)(2,1)} %get-tuple-element.10) | data formatting | bytes 6291456
  67.5 21.6 %all-gather.2.cloned.1.call-done = bf16[128,7680]{1,0:T(8,128)(2,1)} async-done(((bf16[16,7680]{1,0:T(8,128)(2,1)}), bf16[128,7680]{1,0:T(8,128)(2,1)}) %all-gather.2.cloned.1.call-update) | async-done | bytes 1966096 | tf_op jit(solution)/shard_map/all_gather | solution.py:52
  89.1 5.2 %fusion.10 = f32[768,128]{0,1:T(8,128)S(1)} fusion(bf16[768,4096]{1,0:T(8,128)(2,1)} %copy-done.2, bf16[128,7680]{1,0:T(8,128)(2,1)} %all-gather.2.cloned.1.call-done), kind=kOutput, calls=%fused_computation.30 | convolution fusion | flops 805306368 | bytes 7733248 | tf_op jit(solution)/shard_map/dot_general | solution.py:11
  94.4 4.7 fusion.9
  99.1 7.4 %psum.7 = f32[768]{0:T(1024)S(1)} all-reduce(f32[768]{0:T(1024)S(1)} %fusion.9), channel_id=1, replica_groups=mesh['tensor'=4,'dp'=8] {'tensor'}, use_global_device_ids=true, to_apply=%region_3.4 | all-reduce | flops 768 | bytes 6144 | tf_op jit(solution)/shard_map/psum | solution.py:65
  106.6 3.5 collective-permute-start
  110.1 5.3 %constant_dynamic-update-slice_fusion.1 = bf16[1536,3584]{1,0:T(8,128)(2,1)} fusion(bf16[768,3584]{1,0:T(8,128)(2,1)} %param.6), kind=kLoop, calls=%fused_computation.66 | loop fusion | bytes 11010048
  115.4 13.3 %copy.33 = bf16[768,2,1,1024]{0,3,1,2:T(8,128)(2,1)S(1)} copy(bf16[768,2,1,1024]{3,2,1,0:T(2,128)(2,1)} %get-tuple-element.9) | data formatting | bytes 6291456
  128.7 106.6 %collective-permute-done = f32[768]{0:T(1024)S(1)} collective-permute-done((f32[768]{0:T(1024)S(1)}, f32[768]{0:T(1024)S(1)}, u32[]{:S(2)}, u32[]{:S(2)}) %collective-permute-start) | collective-permute-done | bytes 3104 | tf_op jit(solution)/shard_map/ppermute | solution.py:28
  235.3 3.2 multiply_convert_fusion
  238.5 3.3 constant_dynamic-slice_fusion
  241.8 3.5 copy.25
  254.1 3.5 copy.23
  263.8 5.4 %constant_dynamic-update-slice_fusion = bf16[1536,3584]{1,0:T(8,128)(2,1)} fusion(bf16[1536,3584]{1,0:T(8,128)(2,1)} %constant_dynamic-update-slice_fusion.1, bf16[768,3584]{1,0:T(8,128)(2,1)} %collective-permute-done.2), kind=kLoop, calls=%fused_computation.65 | loop fusion | bytes 11010048 | tf_op jit(solution)/shard_map/concatenate | solution.py:78
  269.2 7.3 %convolution_convert_fusion.2 = bf16[256,3584]{1,0:T(8,128)(2,1)S(1)} fusion(bf16[1536,256]{0,1:T(8,128)(2,1)S(1)} %bitcast.81, bf16[1536,3584]{1,0:T(8,128)(2,1)} %constant_dynamic-update-slice_fusion), kind=kOutput, calls=%fused_computation.12 | convolution fusion | flops 2819489792 | bytes 13631488 | tf_op jit(solution)/shard_map/dot_general | solution.py:86
  276.6 3.0 convolution_convert_fusion.3
  281.7 3.0 convolution_convert_fusion
  284.7 3.0 convolution_convert_fusion.1
  289.8 32.8 %collective-permute-done.3 = bf16[256,3584]{1,0:T(8,128)(2,1)S(1)} collective-permute-done((bf16[256,3584]{1,0:T(8,128)(2,1)S(1)}, bf16[256,3584]{1,0:T(8,128)(2,1)S(1)}, u32[]{:S(2)}, u32[]{:S(2)}) %collective-permute-start.3) | collective-permute-done | bytes 1835040 | tf_op jit(solution)/shard_map/ppermute | solution.py:28
  322.6 3.0 fusion
  328.5 33.4 %collective-permute-done.5 = bf16[256,3584]{1,0:T(8,128)(2,1)S(1)} collective-permute-done((bf16[256,3584]{1,0:T(8,128)(2,1)S(1)}, bf16[256,3584]{1,0:T(8,128)(2,1)S(1)}, u32[]{:S(2)}, u32[]{:S(2)}) %collective-permute-start.5) | collective-permute-done | bytes 1835040 | tf_op jit(solution)/shard_map/ppermute | solution.py:28
  362.0 3.3 fusion.1
  368.1 33.2 %collective-permute-done.7 = bf16[256,3584]{1,0:T(8,128)(2,1)S(1)} collective-permute-done((bf16[256,3584]{1,0:T(8,128)(2,1)S(1)}, bf16[256,3584]{1,0:T(8,128)(2,1)S(1)}, u32[]{:S(2)}, u32[]{:S(2)}) %collective-permute-start.7) | collective-permute-done | bytes 1835040 | tf_op jit(solution)/shard_map/ppermute | solution.py:28
  401.3 3.1 fusion.2
  407.2 31.7 %collective-permute-done.9 = bf16[256,3584]{1,0:T(8,128)(2,1)S(1)} collective-permute-done((bf16[256,3584]{1,0:T(8,128)(2,1)S(1)}, bf16[256,3584]{1,0:T(8,128)(2,1)S(1)}, u32[]{:S(2)}, u32[]{:S(2)}) %collective-permute-start.9) | collective-permute-done | bytes 1835040 | tf_op jit(solution)/shard_map/ppermute | solution.py:28
  438.9 3.1 fusion.3
  445.2 38.3 %collective-permute-done.10 = bf16[128,3584]{1,0:T(8,128)(2,1)S(1)} collective-permute-done((bf16[128,3584]{1,0:T(8,128)(2,1)S(1)}, bf16[128,3584]{1,0:T(8,128)(2,1)S(1)}, u32[]{:S(2)}, u32[]{:S(2)}) %collective-permute-start.10) | collective-permute-done | bytes 917536 | tf_op jit(solution)/shard_map/ppermute | solution.py:28
  (74 shorter events, 40.8 us)
Async XLA Ops:
  6.5 1.6 copy-start
  6.5 6.5 %copy-start.13 = (bf16[14,4096]{1,0:T(8,128)(2,1)S(1)}, bf16[14,4096]{1,0:T(8,128)(2,1)}, u32[]{:S(2)}) copy-start(bf16[14,4096]{1,0:T(8,128)(2,1)} %param.8) | copy-start | bytes 344068
  6.5 82.6 %all-gather.2.cloned.1.call-start = ((), (), s32[]{:S(2)}) async-start(), calls=%async_computation | async-start | bytes 2211840 | tf_op jit(solution)/shard_map/all_gather | solution.py:52
  17.7 2.6 copy-start.2
  22.0 241.7 %collective-permute-start.2 = (bf16[768,3584]{1,0:T(8,128)(2,1)}, bf16[768,3584]{1,0:T(8,128)(2,1)}, u32[]{:S(2)}, u32[]{:S(2)}) collective-permute-start(bf16[768,3584]{1,0:T(8,128)(2,1)} %param.6), channel_id=1, source_target_pairs={{0,2},{1,3},{2,0},{3,1},{4,6},{5,7},{6,4},{7,5},{8,10},{9,11},{10,... | collective-permute-start | bytes 16515080 | tf_op jit(solution)/shard_map/ppermute | solution.py:28
  67.4 167.9 %collective-permute-start.1 = (bf16[768,2048]{0,1:T(8,128)(2,1)}, bf16[768,2048]{0,1:T(8,128)(2,1)}, u32[]{:S(2)}, u32[]{:S(2)}) collective-permute-start(bf16[768,2048]{0,1:T(8,128)(2,1)} %bitcast.2), channel_id=1, source_target_pairs={{0,2},{1,3},{2,0},{3,1},{4,6},{5,7},{6,4},{7,5},{8,10},{9,11},{10,... | collective-permute-start | bytes 9437192 | tf_op jit(solution)/shard_map/ppermute | solution.py:28
  94.4 12.2 %copy-start.14 = (s32[768]{0:T(1024)S(1)}, s32[768]{0:T(1024)}, u32[]{:S(2)}) copy-start(s32[768]{0:T(1024)} %param.11) | copy-start | bytes 9220
  106.6 128.7 %collective-permute-start = (f32[768]{0:T(1024)S(1)}, f32[768]{0:T(1024)S(1)}, u32[]{:S(2)}, u32[]{:S(2)}) collective-permute-start(f32[768]{0:T(1024)S(1)} %fusion.31), channel_id=1, source_target_pairs={{0,2},{1,3},{2,0},{3,1},{4,6},{5,7},{6,4},{7,5},{8,10},{9,11},{10,... | collective-permute-start | bytes 9224 | tf_op jit(solution)/shard_map/ppermute | solution.py:28
  247.0 4.7 copy-start.5
  247.0 5.9 %copy-start.3 = (bf16[1536,2,1,128]{3,0,2,1:T(8,128)(2,1)S(1)}, bf16[1536,2,1,128]{3,0,2,1:T(8,128)(2,1)}, u32[]{:S(2)}) copy-start(bf16[1536,2,1,128]{3,0,2,1:T(8,128)(2,1)} %get-tuple-element.14) | copy-start | bytes 2359300
  259.3 3.8 copy-start.6
  259.3 4.1 copy-start.4
  263.7 5.5 %copy-start.12 = (bf16[1536,2,1,128]{0,3,1,2:T(8,128)(2,1)S(1)}, bf16[1536,2,1,128]{0,3,1,2:T(8,128)(2,1)}, u32[]{:S(2)}) copy-start(bf16[1536,2,1,128]{0,3,1,2:T(8,128)(2,1)} %copy.28) | copy-start | bytes 2359300
  269.2 7.3 %copy-start.7 = (bf16[1536,3584]{1,0:T(8,128)(2,1)S(1)}, bf16[1536,3584]{1,0:T(8,128)(2,1)}, u32[]{:S(2)}) copy-start(bf16[1536,3584]{1,0:T(8,128)(2,1)} %constant_dynamic-update-slice_fusion) | copy-start | bytes 33030148
  269.2 7.4 %copy-start.11 = (bf16[1536,2,1,128]{0,3,1,2:T(8,128)(2,1)S(1)}, bf16[1536,2,1,128]{0,3,1,2:T(8,128)(2,1)}, u32[]{:S(2)}) copy-start(bf16[1536,2,1,128]{0,3,1,2:T(8,128)(2,1)} %copy.26) | copy-start | bytes 2359300
  276.6 5.1 %copy-start.8 = (bf16[1536,2,1,128]{0,3,1,2:T(8,128)(2,1)S(1)}, bf16[1536,2,1,128]{0,3,1,2:T(8,128)(2,1)}, u32[]{:S(2)}) copy-start(bf16[1536,2,1,128]{0,3,1,2:T(8,128)(2,1)} %copy.32) | copy-start | bytes 2359300
  279.6 43.0 %collective-permute-start.3 = (bf16[256,3584]{1,0:T(8,128)(2,1)S(1)}, bf16[256,3584]{1,0:T(8,128)(2,1)S(1)}, u32[]{:S(2)}, u32[]{:S(2)}) collective-permute-start(bf16[256,3584]{1,0:T(8,128)(2,1)S(1)} %convolution_convert_fusion.3), channel_id=1, source_target_pairs={{0,1},{1,0},{2,3},{3,2},{4,5},{5,4},{6,7},{7,6},{8,9},{9,8},{10,11... | collective-permute-start | bytes 5505032 | tf_op jit(solution)/shard_map/ppermute | solution.py:28
  281.3 80.6 %collective-permute-start.5 = (bf16[256,3584]{1,0:T(8,128)(2,1)S(1)}, bf16[256,3584]{1,0:T(8,128)(2,1)S(1)}, u32[]{:S(2)}, u32[]{:S(2)}) collective-permute-start(bf16[256,3584]{1,0:T(8,128)(2,1)S(1)} %convolution_convert_fusion.2), channel_id=1, source_target_pairs={{0,1},{1,0},{2,3},{3,2},{4,5},{5,4},{6,7},{7,6},{8,9},{9,8},{10,11... | collective-permute-start | bytes 5505032 | tf_op jit(solution)/shard_map/ppermute | solution.py:28
  281.7 3.0 copy-start.9
  284.7 37.9 %copy-start.10 = (bf16[1536,2,1,128]{0,3,1,2:T(8,128)(2,1)S(1)}, bf16[1536,2,1,128]{0,3,1,2:T(8,128)(2,1)}, u32[]{:S(2)}) copy-start(bf16[1536,2,1,128]{0,3,1,2:T(8,128)(2,1)} %copy.24) | copy-start | bytes 2359300
  287.8 113.5 %collective-permute-start.7 = (bf16[256,3584]{1,0:T(8,128)(2,1)S(1)}, bf16[256,3584]{1,0:T(8,128)(2,1)S(1)}, u32[]{:S(2)}, u32[]{:S(2)}) collective-permute-start(bf16[256,3584]{1,0:T(8,128)(2,1)S(1)} %convolution_convert_fusion.1), channel_id=1, source_target_pairs={{0,1},{1,0},{2,3},{3,2},{4,5},{5,4},{6,7},{7,6},{8,9},{9,8},{10,11... | collective-permute-start | bytes 5505032 | tf_op jit(solution)/shard_map/ppermute | solution.py:28
  289.5 149.4 %collective-permute-start.9 = (bf16[256,3584]{1,0:T(8,128)(2,1)S(1)}, bf16[256,3584]{1,0:T(8,128)(2,1)S(1)}, u32[]{:S(2)}, u32[]{:S(2)}) collective-permute-start(bf16[256,3584]{1,0:T(8,128)(2,1)S(1)} %convolution_convert_fusion), channel_id=1, source_target_pairs={{0,1},{1,0},{2,3},{3,2},{4,5},{5,4},{6,7},{7,6},{8,9},{9,8},{10,11... | collective-permute-start | bytes 5505032 | tf_op jit(solution)/shard_map/ppermute | solution.py:28
  325.7 118.8 %collective-permute-start.4 = (bf16[128,3584]{1,0:T(8,128)(2,1)S(1)}, bf16[128,3584]{1,0:T(8,128)(2,1)S(1)}, u32[]{:S(2)}, u32[]{:S(2)}) collective-permute-start(bf16[128,3584]{1,0:T(8,128)(2,1)S(1)} %dynamic-slice_bitcast_fusion.3), channel_id=1, source_target_pairs={{0,4},{1,5},{2,6},{3,7},{4,0},{5,1},{6,2},{7,3},{8,12},{9,13},{10,... | collective-permute-start | bytes 2752520 | tf_op jit(solution)/shard_map/ppermute | solution.py:28
  365.3 79.4 %collective-permute-start.6 = (bf16[128,3584]{1,0:T(8,128)(2,1)S(1)}, bf16[128,3584]{1,0:T(8,128)(2,1)S(1)}, u32[]{:S(2)}, u32[]{:S(2)}) collective-permute-start(bf16[128,3584]{1,0:T(8,128)(2,1)S(1)} %dynamic-slice_bitcast_fusion.2), channel_id=1, source_target_pairs={{0,4},{1,5},{2,6},{3,7},{4,0},{5,1},{6,2},{7,3},{8,12},{9,13},{10,... | collective-permute-start | bytes 2752520 | tf_op jit(solution)/shard_map/ppermute | solution.py:28
  404.4 40.6 %collective-permute-start.8 = (bf16[128,3584]{1,0:T(8,128)(2,1)S(1)}, bf16[128,3584]{1,0:T(8,128)(2,1)S(1)}, u32[]{:S(2)}, u32[]{:S(2)}) collective-permute-start(bf16[128,3584]{1,0:T(8,128)(2,1)S(1)} %dynamic-slice_bitcast_fusion.1), channel_id=1, source_target_pairs={{0,4},{1,5},{2,6},{3,7},{4,0},{5,1},{6,2},{7,3},{8,12},{9,13},{10,... | collective-permute-start | bytes 2752520 | tf_op jit(solution)/shard_map/ppermute | solution.py:28
  442.0 41.5 %collective-permute-start.10 = (bf16[128,3584]{1,0:T(8,128)(2,1)S(1)}, bf16[128,3584]{1,0:T(8,128)(2,1)S(1)}, u32[]{:S(2)}, u32[]{:S(2)}) collective-permute-start(bf16[128,3584]{1,0:T(8,128)(2,1)S(1)} %dynamic-slice_bitcast_fusion), channel_id=1, source_target_pairs={{0,4},{1,5},{2,6},{3,7},{4,0},{5,1},{6,2},{7,3},{8,12},{9,13},{10,... | collective-permute-start | bytes 2752520 | tf_op jit(solution)/shard_map/ppermute | solution.py:28
  483.5 2.2 copy-start.1
Sparse Core Ops, SparseCore 0:
  22.2 66.9 all-gather.1
